TPU v7x, 32 devices: a whole 2x2x4 slice. The times are simulated.
32 devices in a mesh: group: 2 (over x), row: 16 (over z, y, core).
Axes of the slice: x: 2, y: 2, z: 4, core: 2. Of those that a mesh axis runs over, the one named last changes fastest.
Arguments:
- pair_input: bfloat16 [256, 128, 128], P(('group', 'row')), parts along dimension 0, may hold values from -6 to 6
- tri_projection: bfloat16 [128, 512], replicated, may hold values from -0.5 to 0.5
- tri_gate_weight: bfloat16 [128, 128], replicated, may hold values from -0.5 to 0.5
- tri_out_weight: bfloat16 [128, 128], replicated, may hold values from -0.5 to 0.5
- pair_bias_weight: bfloat16 [128, 4], replicated
- atom_input: bfloat16 [2048, 128], P(('group', 'row')), parts along dimension 0, may hold values from -6 to 6
- atom_tokens: int32 [2048], P('group'), parts along dimension 0, may hold values from 0 to 127, as said below
- atom_in_weight: bfloat16 [128, 512], replicated, may hold values from -0.5 to 0.5
- atom_out_weight: bfloat16 [128, 128], replicated, may hold values from -0.5 to 0.5
Outputs:
- pair_output: bfloat16 [256, 128, 128], P(('group', 'row')), parts along dimension 0
- atom_output: bfloat16 [2048, 128], P(('group', 'row')), parts along dimension 0
There are 2 independent parts, one for each index of `group`. A program takes and returns all parts, laid end to end along the dimension named above; an argument that names none is the same for every part. Nothing has to cross between parts.
Inputs may be any that keep to these rules, and one draw needn't show every extreme that they name: `atom_tokens`: never falls along the atoms; atoms 64 q to 64 q + 63 belong to tokens 8 q to 8 q + 7, each of these tokens has 1 to 24 of them.
All inputs are finite; a program needn't handle non-finite values.
Results may differ from a plain program's by a relative error of at most 0.012.
Values may be sent and summed in bfloat16 or wider, within the bound.
A program may use at most 192 MiB of HBM per device.

v0:
```python
import jax
import jax.numpy as jnp
from jax import lax
from jax.sharding import PartitionSpec as P

QB = 32
KB = 128
RIM = 48


NORM_EPSILON = 1e-05


def padded(block, sides, width):
    for axis, dim in sides:
        count = lax.axis_size(axis)
        forward = [(i, i + 1) for i in range(count - 1)]
        backward = [(target, source) for source, target in forward]
        low = lax.ppermute(
            lax.slice_in_dim(block, block.shape[dim] - width, None, axis=dim), axis, forward
        )
        high = lax.ppermute(lax.slice_in_dim(block, 0, width, axis=dim), axis, backward)
        block = jnp.concatenate([low, block, high], axis=dim)
    return block


def layer_norm(values, axis):
    average = jnp.mean(values, axis=axis, keepdims=True)
    centred = values - average
    variance = jnp.mean(centred * centred, axis=axis, keepdims=True)
    return centred * lax.rsqrt(variance + NORM_EPSILON)


def windows(blocked, count):
    return jnp.concatenate([blocked[offset : offset + count] for offset in range(KB // QB)], axis=1)


def per_device(
    pair_input,
    tri_projection,
    tri_gate_weight,
    tri_out_weight,
    pair_bias_weight,
    atom_input,
    atom_tokens,
    atom_in_weight,
    atom_out_weight,
):
    rows_here, token_count, pair_width = pair_input.shape
    normed = layer_norm(pair_input.astype(jnp.float32), -1).astype(jnp.bfloat16)
    projected = jnp.einsum(
        "kid,de->eki", normed, tri_projection, preferred_element_type=jnp.float32
    )
    left_side = (
        jax.nn.sigmoid(projected[pair_width : 2 * pair_width]) * projected[:pair_width]
    ).astype(jnp.bfloat16)
    right_side = (
        jax.nn.sigmoid(projected[3 * pair_width :]) * projected[2 * pair_width : 3 * pair_width]
    ).astype(jnp.bfloat16)
    gate_out = jax.nn.sigmoid(
        jnp.einsum("kid,de->kie", normed, tri_gate_weight, preferred_element_type=jnp.float32)
    )
    turned = lax.all_to_all(left_side, "row", split_axis=2, concat_axis=1, tiled=True)
    triangle = jnp.einsum(
        "cki,ckj->cij",
        turned,
        lax.all_gather(right_side, "row", axis=1, tiled=True),
        preferred_element_type=jnp.float32,
    )
    tri_normed = layer_norm(triangle, 0).astype(jnp.bfloat16)
    update = jnp.einsum(
        "cij,cd->ijd", tri_normed, tri_out_weight, preferred_element_type=jnp.float32
    )
    pair_output = (pair_input.astype(jnp.float32) + gate_out * update).astype(jnp.bfloat16)
    pair_normed = layer_norm(pair_output.astype(jnp.float32), -1).astype(jnp.bfloat16)
    bias_rows = jnp.einsum(
        "ijc,ch->hij", pair_normed, pair_bias_weight, preferred_element_type=jnp.float32
    )
    atom_count, atom_width = atom_input.shape
    total_atoms = atom_tokens.shape[0]
    head_count = pair_bias_weight.shape[1]
    head_size = atom_width // head_count
    block_count = atom_count // QB
    atom_normed = layer_norm(atom_input.astype(jnp.float32), -1).astype(jnp.bfloat16)
    atom_proj = jnp.dot(atom_normed, atom_in_weight, preferred_element_type=jnp.float32)
    queries = (atom_proj[:, :atom_width] * head_size ** (-0.5)).astype(jnp.bfloat16)
    queries = queries.reshape(block_count, QB, head_count, head_size)
    key_value = atom_proj[:, atom_width : 3 * atom_width].astype(jnp.bfloat16)
    gating = jax.nn.sigmoid(atom_proj[:, 3 * atom_width :])
    extended = padded(key_value, (("row", 0),), RIM)
    key_windows = windows(extended.reshape(-1, QB, 2 * atom_width), block_count)
    keys = key_windows[:, :, :atom_width].reshape(block_count, KB, head_count, head_size)
    values_win = key_windows[:, :, atom_width:].reshape(block_count, KB, head_count, head_size)
    device_index = lax.axis_index("row")
    first_atom = device_index * atom_count
    first_row = device_index * rows_here
    positions = first_atom - RIM + jnp.arange(atom_count + 2 * RIM, dtype=jnp.int32)
    inside = windows(((positions >= 0) & (positions < total_atoms)).reshape(-1, QB), block_count)
    padded_tokens = jnp.pad(atom_tokens, RIM)
    key_tokens = lax.dynamic_slice_in_dim(padded_tokens, first_atom, atom_count + 2 * RIM)
    query_tokens = lax.dynamic_slice_in_dim(atom_tokens, first_atom, atom_count) - first_row
    token_ids = jnp.arange(token_count, dtype=jnp.int32)
    row_ids = jnp.arange(rows_here, dtype=jnp.int32)
    query_hot = (query_tokens[:, None] == row_ids[None, :]).astype(jnp.float32)
    key_hot = (key_tokens[:, None] == token_ids[None, :]).astype(jnp.float32)
    bias_queries = jnp.einsum("lt,hts->hls", query_hot, bias_rows, precision=lax.Precision.HIGHEST)
    bias_queries = bias_queries.reshape(head_count, block_count, QB, token_count)
    key_hot_win = windows(key_hot.reshape(-1, QB, token_count), block_count)
    bias = jnp.einsum("hbls,bms->bhlm", bias_queries, key_hot_win, precision=lax.Precision.HIGHEST)
    scores = jnp.einsum("blhd,bmhd->bhlm", queries, keys, preferred_element_type=jnp.float32) + bias
    scores = jnp.where(inside[:, None, None, :], scores, -jnp.inf)
    maxima = jnp.max(scores, axis=-1, keepdims=True)
    powers = jnp.exp(scores - maxima)
    weights = (powers / jnp.sum(powers, axis=-1, keepdims=True)).astype(jnp.bfloat16)
    attended = jnp.einsum(
        "bhlm,bmhd->blhd", weights, values_win, preferred_element_type=jnp.float32
    )
    attended = attended.reshape(atom_count, atom_width)
    gated = (gating * attended).astype(jnp.bfloat16)
    projected_out = jnp.dot(gated, atom_out_weight, preferred_element_type=jnp.float32)
    atom_output = (projected_out + atom_input.astype(jnp.float32)).astype(jnp.bfloat16)
    return (pair_output, atom_output)


def solution(mesh):
    placed = (
        P(("group", "row"), None, None),
        P(),
        P(),
        P(),
        P(),
        P(("group", "row"), None),
        P("group"),
        P(),
        P(),
    )
    return jax.shard_map(
        per_device,
        mesh=mesh,
        in_specs=placed,
        out_specs=(P(("group", "row"), None, None), P(("group", "row"), None)),
        check_vma=False,
    )
```

profile of v0, /device:TPU:0, one launch (start us, length us, event | category | flops | bytes accessed | tf_op | source)
XLA Modules:
  0.0 83.5 jit_solution(1858786012426279319)
XLA Ops:
  7.3 1.2 %copy.58 = bf16[8,128,128]{1,2,0:T(8,128)(2,1)S(1)} copy(bf16[8,128,128]{2,1,0:T(8,128)(2,1)} %param.9) | data formatting | bytes 524288 | tf_op args[0]
  8.6 0.5 convolution_bitcast_fusion
  9.1 0.3 fusion.20
  9.4 0.8 copy.65
  10.2 0.9 %copy.62 = bf16[128,8,128]{0,1,2:T(8,128)(2,1)} copy(bf16[128,8,128]{0,2,1:T(8,128)(2,1)S(1)} %get-tuple-element.11) | data formatting | bytes 524288 | tf_op jit(solution)/shard_map/convert_element_type | solution.py:56
  11.1 7.4 %all-to-all-start = ((bf16[128,8,128]{0,1,2:T(8,128)(2,1)}), bf16[128,8,128]{0,1,2:T(8,128)(2,1)S(1)}, u32[]{:S(2)}, u32[]{:S(2)}) async-start(bf16[128,8,128]{0,1,2:T(8,128)(2,1)} %copy.62), calls=%async_computation | async-start | bytes 524288 | tf_op jit(solution)/shard_map/all_to_all | solution.py:63
  18.6 0.2 fusion.48
  18.8 0.2 fusion.83
  19.1 2.3 %collective-permute-start = (bf16[48,256]{1,0:T(8,128)(2,1)S(1)}, bf16[48,256]{1,0:T(8,128)(2,1)S(1)}, u32[]{:S(2)}, u32[]{:S(2)}) collective-permute-start(bf16[48,256]{1,0:T(8,128)(2,1)S(1)} %get-tuple-element.18), channel_id=1, source_target_pairs={{0,1},{1,2},{2,3},{3,4},{4,5},{5,6},{6,7},{7,8},{8,9},{9,10},{10,1... | collective-permute-start | bytes 73736 | tf_op jit(solution)/shard_map/ppermute | solution.py:19
  21.4 1.3 %collective-permute-start.1 = (bf16[48,256]{1,0:T(8,128)(2,1)S(1)}, bf16[48,256]{1,0:T(8,128)(2,1)S(1)}, u32[]{:S(2)}, u32[]{:S(2)}) collective-permute-start(bf16[48,256]{1,0:T(8,128)(2,1)S(1)} %get-tuple-element.19), channel_id=1, source_target_pairs={{1,0},{2,1},{3,2},{4,3},{5,4},{6,5},{7,6},{8,7},{9,8},{10,9},{11,1... | collective-permute-start | bytes 73736 | tf_op jit(solution)/shard_map/ppermute | solution.py:22
  23.0 0.3 fusion.5
  23.6 2.0 %collective-permute-done.1 = bf16[48,256]{1,0:T(8,128)(2,1)S(1)} collective-permute-done((bf16[48,256]{1,0:T(8,128)(2,1)S(1)}, bf16[48,256]{1,0:T(8,128)(2,1)S(1)}, u32[]{:S(2)}, u32[]{:S(2)}) %collective-permute-start.1) | collective-permute-done | bytes 24608 | tf_op jit(solution)/shard_map/ppermute | solution.py:22
  25.9 4.9 %all-to-all-done = bf16[128,8,128]{0,1,2:T(8,128)(2,1)S(1)} async-done(((bf16[128,8,128]{0,1,2:T(8,128)(2,1)}), bf16[128,8,128]{0,1,2:T(8,128)(2,1)S(1)}, u32[]{:S(2)}, u32[]{:S(2)}) %all-to-all-start) | async-done | bytes 262176 | tf_op jit(solution)/shard_map/all_to_all | solution.py:63
  30.8 0.2 copy.66
  31.1 35.7 %all-gather.2.cloned.1.call-done = bf16[128,128,128]{2,0,1:T(8,128)(2,1)} async-done(((bf16[128,8,128]{2,0,1:T(8,128)(2,1)}), bf16[128,128,128]{2,0,1:T(8,128)(2,1)}) %all-gather.2.cloned.1.call-update) | async-done | bytes 4194320 | tf_op jit(solution)/shard_map/all_gather | solution.py:67
  66.8 5.6 %fusion.82 = (f32[8,128]{1,0:T(8,128)S(1)}, f32[128,8,128]{2,1,0:T(8,128)S(1)}) fusion(bf16[128,128,8]{1,2,0:T(8,128)(2,1)S(1)} %copy.66, bf16[128,128,128]{2,0,1:T(8,128)(2,1)} %all-gather.2.cloned.1.call-done), kind=kOutput, calls=%fused_computation.120 | convolution fusion | flops 33684480 | bytes 4984832 | tf_op jit(solution)/shard_map/cki,ckj->cij/dot_general | solution.py:64
  72.7 0.3 convert_reduce_fusion.1
  73.0 0.9 %copy.77 = bf16[8,128,128]{2,1,0:T(8,128)(2,1)} copy(bf16[8,128,128]{1,2,0:T(8,128)(2,1)S(1)} %get-tuple-element.35) | data formatting | bytes 524288
  74.0 0.2 convolution_bitcast_fusion.2
  74.1 0.3 fusion.63
  74.4 0.4 fusion.34
  75.0 0.2 fusion.84
  75.2 0.5 convolution_bitcast_fusion.1
  75.9 0.7 fusion.11
  (53 shorter events, 1.8 us)
Async XLA Ops:
  7.2 1.5 %copy-start = (bf16[128,512]{1,0:T(8,128)(2,1)S(1)}, bf16[128,512]{1,0:T(8,128)(2,1)}, u32[]{:S(2)}) copy-start(bf16[128,512]{1,0:T(8,128)(2,1)} %param.10) | copy-start | bytes 393220
  7.2 11.3 %copy-start.1 = (bf16[64,128]{1,0:T(8,128)(2,1)S(1)}, bf16[64,128]{1,0:T(8,128)(2,1)}, u32[]{:S(2)}) copy-start(bf16[64,128]{1,0:T(8,128)(2,1)} %param.14) | copy-start | bytes 49156
  7.2 11.6 %copy-start.2 = (bf16[128,512]{1,0:T(8,128)(2,1)S(1)}, bf16[128,512]{1,0:T(8,128)(2,1)}, u32[]{:S(2)}) copy-start(bf16[128,512]{1,0:T(8,128)(2,1)} %param.16) | copy-start | bytes 393220
  7.2 15.5 %copy-start.4 = (s32[1024]{0:T(1024)S(1)}, s32[1024]{0:T(1024)}, u32[]{:S(2)}) copy-start(s32[1024]{0:T(1024)} %param.15) | copy-start | bytes 12292
  7.2 59.6 %all-gather.2.cloned.1.call-start = ((), (), s32[]{:S(2)}) async-start(), calls=%async_computation.1 | async-start | bytes 4456448 | tf_op jit(solution)/shard_map/all_gather | solution.py:67
  8.5 14.6 %copy-start.5 = (bf16[128,128]{1,0:T(8,128)(2,1)S(1)}, bf16[128,128]{1,0:T(8,128)(2,1)}, u32[]{:S(2)}) copy-start(bf16[128,128]{1,0:T(8,128)(2,1)} %param.11) | copy-start | bytes 98308
  11.1 19.7 %all-to-all-start = ((bf16[128,8,128]{0,1,2:T(8,128)(2,1)}), bf16[128,8,128]{0,1,2:T(8,128)(2,1)S(1)}, u32[]{:S(2)}, u32[]{:S(2)}) async-start(bf16[128,8,128]{0,1,2:T(8,128)(2,1)} %copy.62), calls=%async_computation | async-start | bytes 524288 | tf_op jit(solution)/shard_map/all_to_all | solution.py:63
  19.1 4.5 %collective-permute-start = (bf16[48,256]{1,0:T(8,128)(2,1)S(1)}, bf16[48,256]{1,0:T(8,128)(2,1)S(1)}, u32[]{:S(2)}, u32[]{:S(2)}) collective-permute-start(bf16[48,256]{1,0:T(8,128)(2,1)S(1)} %get-tuple-element.18), channel_id=1, source_target_pairs={{0,1},{1,2},{2,3},{3,4},{4,5},{5,6},{6,7},{7,8},{8,9},{9,10},{10,1... | collective-permute-start | bytes 73736 | tf_op jit(solution)/shard_map/ppermute | solution.py:19
  21.4 4.2 %collective-permute-start.1 = (bf16[48,256]{1,0:T(8,128)(2,1)S(1)}, bf16[48,256]{1,0:T(8,128)(2,1)S(1)}, u32[]{:S(2)}, u32[]{:S(2)}) collective-permute-start(bf16[48,256]{1,0:T(8,128)(2,1)S(1)} %get-tuple-element.19), channel_id=1, source_target_pairs={{1,0},{2,1},{3,2},{4,3},{5,4},{6,5},{7,6},{8,7},{9,8},{10,9},{11,1... | collective-permute-start | bytes 73736 | tf_op jit(solution)/shard_map/ppermute | solution.py:22
  23.5 49.1 %copy-start.3 = (bf16[128,128]{1,0:T(8,128)(2,1)S(1)}, bf16[128,128]{1,0:T(8,128)(2,1)}, u32[]{:S(2)}) copy-start(bf16[128,128]{1,0:T(8,128)(2,1)} %param.12) | copy-start | bytes 98308
  31.1 42.9 %copy-start.7 = (bf16[128,4]{0,1:T(4,128)(2,1)S(1)}, bf16[128,4]{0,1:T(4,128)(2,1)}, u32[]{:S(2)}) copy-start(bf16[128,4]{0,1:T(4,128)(2,1)} %param.13) | copy-start | bytes 3076
  72.5 3.4 %copy-start.6 = (bf16[128,128]{1,0:T(8,128)(2,1)S(1)}, bf16[128,128]{1,0:T(8,128)(2,1)}, u32[]{:S(2)}) copy-start(bf16[128,128]{1,0:T(8,128)(2,1)} %param.17) | copy-start | bytes 98308
Sparse Core Ops, SparseCore 0:
  10.4 56.4 all-gather.1
where the time goes:
time: 83.8 us; the launch traced here: 83.5 us
  waiting for transfers between devices  42.6 us (51%)
  between operations  14.4 us (17%)
  starting transfers between devices  11 us (13%)
  matrix products  9.17 us (11%)
  local copies, waits for them, and re-layouts  4.78 us (6%)
  other arithmetic  1.49 us (2%)
    all_gather x1, waiting for transfers between devices, per_device(): lax.all_gather(right_side, 'row', axis=1, tiled=True)  35.7 us
    all_to_all x1, starting transfers between devices, per_device(): lax.all_to_all(left_side, 'row', split_axis=2, concat_axis=1, tiled=True)  7.38 us
    dot_general x1, matrix products, per_device(): jnp.einsum('cki,ckj->cij', turned, lax.all_gather(right_side, 'row', axis...  5.63 us
    all_to_all x1, waiting for transfers between devices, per_device(): lax.all_to_all(left_side, 'row', split_axis=2, concat_axis=1, tiled=True)  4.86 us
    ppermute x1, starting transfers between devices, padded(): lax.ppermute(lax.slice_in_dim(block, block.shape[dim] - width, None, axis...  2.31 us
    unnamed x18, local copies, waits for them, and re-layouts  2.09 us
    ppermute x1, waiting for transfers between devices, padded(): lax.ppermute(lax.slice_in_dim(block, 0, width, axis=dim), axis, backward)  2.05 us
  transfers between devices with their start and end apart: 4, of which 3 were waited for; matrix products, arithmetic and copies ran while one was open for 3% of the time, Pallas kernels for 0%

commit v1 on v0

v1 whole, which is shorter than its diff:
```python
import functools

import jax
import jax.numpy as jnp
from jax import lax
from jax.experimental import pallas as pl
from jax.experimental.pallas import tpu as pltpu
from jax.sharding import PartitionSpec as P

QB = 32
KB = 128
RIM = 48
LANES = 128
NORM_EPSILON = 1e-05
F32 = jnp.float32
BF16 = jnp.bfloat16
NN = (((1,), (0,)), ((), ()))
NT = (((1,), (1,)), ((), ()))


def dot(a, b, dims=NN):
    return lax.dot_general(a, b, dims, preferred_element_type=F32)


def turned(x):
    return jnp.transpose(x.astype(F32)).astype(BF16)


def layer_norm(values, axis):
    average = jnp.mean(values, axis=axis, keepdims=True)
    centred = values - average
    variance = jnp.mean(centred * centred, axis=axis, keepdims=True)
    return centred * lax.rsqrt(variance + NORM_EPSILON)


def kernel(
    count,
    total_atoms,
    pair_ref,
    proj_ref,
    gate_ref,
    out_ref,
    bias_ref,
    atom_ref,
    qtok_ref,
    ktok_ref,
    ain_ref,
    aout_ref,
    pair_out,
    atom_out,
    flat_l,
    flat_r,
    send1,
    recv1,
    send2,
    recv2,
    gates,
    ext,
    ssem1,
    rsem1,
    ssem2,
    rsem2,
    hsem_s,
    hsem_r,
):
    rows, tokens, width = pair_ref.shape
    share = width // count
    part = share * rows
    chunks = tokens // LANES
    atoms = atom_ref.shape[0]
    heads = bias_ref.shape[1]
    head_size = width // heads
    blocks = atoms // QB
    me = lax.axis_index("row")
    right = lax.rem(me + 1, count)
    left = lax.rem(me + count - 1, count)

    barrier = pltpu.get_barrier_semaphore()

    def greet(step, carry):
        pl.semaphore_signal(barrier, inc=1, device_id={"row": lax.rem(me + step, count)})
        return carry

    lax.fori_loop(1, count, greet, 0)

    turned_proj = turned(proj_ref[...])
    for k in range(rows):
        normed = layer_norm(pair_ref[k].astype(F32), -1).astype(BF16)
        projected = dot(turned_proj, normed, NT)
        left_side = jax.nn.sigmoid(projected[width : 2 * width]) * projected[:width]
        right_side = jax.nn.sigmoid(projected[3 * width :]) * projected[2 * width : 3 * width]
        for q in range(chunks):
            cut = slice(q * LANES, (q + 1) * LANES)
            flat_l[q, pl.ds(k, width, stride=rows), :] = left_side[:, cut]
            flat_r[q, pl.ds(k, width, stride=rows), :] = right_side[:, cut]
    for q in range(chunks):
        cut = slice(q * LANES, (q + 1) * LANES)
        send1[:, :part, cut] = flat_l[q].reshape(count, part, LANES).astype(BF16)
        send1[:, part:, cut] = flat_r[q].reshape(count, part, LANES).astype(BF16)

    pl.semaphore_wait(barrier, count - 1)

    def halo(side):
        source = atom_ref.at[pl.ds(atoms - RIM, RIM)] if side == 0 else atom_ref.at[pl.ds(0, RIM)]
        target = ext.at[pl.ds(0, RIM)] if side == 0 else ext.at[pl.ds(RIM + atoms, RIM)]
        return pltpu.make_async_remote_copy(
            src_ref=source,
            dst_ref=target,
            send_sem=hsem_s.at[side],
            recv_sem=hsem_r.at[side],
            device_id={"row": right if side == 0 else left},
        )

    def copy1(peer, slot):
        return pltpu.make_async_remote_copy(
            src_ref=send1.at[peer],
            dst_ref=recv1.at[slot],
            send_sem=ssem1.at[peer],
            recv_sem=rsem1.at[slot],
            device_id={"row": peer},
        )

    def copy2(peer, slot):
        return pltpu.make_async_remote_copy(
            src_ref=send2.at[peer],
            dst_ref=recv2.at[slot],
            send_sem=ssem2.at[peer],
            recv_sem=rsem2.at[slot],
            device_id={"row": peer},
        )

    def start1(step, carry):
        copy1(lax.rem(me + step, count), me).start()
        return carry

    def start2(step, carry):
        copy2(lax.rem(me + step, count), me).start()
        return carry

    def wait1(step, carry):
        peer = lax.rem(me + step, count)
        copy1(peer, peer).wait_recv()
        return carry

    def wait2(step, carry):
        peer = lax.rem(me + step, count)
        copy2(peer, peer).wait_recv()
        return carry

    def drain(step, carry):
        peer = lax.rem(me + step, count)
        copy1(peer, peer).wait_send()
        copy2(peer, peer).wait_send()
        return carry

    halo(0).start()
    halo(1).start()
    lax.fori_loop(1, count, start1, 0)
    recv1[me] = send1[me]
    ext[pl.ds(RIM, atoms), :] = atom_ref[...]

    for k in range(rows):
        normed = layer_norm(pair_ref[k].astype(F32), -1).astype(BF16)
        gates[k] = jax.nn.sigmoid(dot(normed, gate_ref[...]))

    halo(0).wait()
    halo(1).wait()
    reach = atoms + 2 * RIM
    atom_normed = layer_norm(ext[...].astype(F32), -1).astype(BF16)
    atom_proj = dot(atom_normed, ain_ref[...])
    own = atom_proj[RIM : RIM + atoms]
    queries = (own[:, :width] * head_size ** (-0.5)).astype(BF16)
    gating = jax.nn.sigmoid(own[:, 3 * width :])
    keys = atom_proj[:, width : 2 * width].astype(BF16)
    vals = atom_proj[:, 2 * width : 3 * width].astype(BF16)
    channel = lax.broadcasted_iota(jnp.int32, (QB, width), 1) // head_size
    first_atom = me * atoms
    key_tokens = ktok_ref[...]
    query_tokens = qtok_ref[...]
    key_hot = (lax.broadcasted_iota(jnp.int32, (tokens, reach), 0) == key_tokens).astype(BF16)
    base = []
    spread = []
    for b in range(blocks):
        q_b = queries[b * QB : (b + 1) * QB]
        q_all = jnp.concatenate(
            [jnp.where(channel == h, q_b, jnp.zeros_like(q_b)) for h in range(heads)], axis=0
        )
        scores = dot(q_all, keys[b * QB : b * QB + KB], NT)
        position = (
            first_atom
            + (b * QB - RIM)
            + lax.broadcasted_iota(jnp.int32, (heads * QB, KB), 1)
        )
        inside = (position >= 0) & (position < total_atoms)
        base.append(jnp.where(inside, scores, -jnp.inf))
        row = lax.broadcasted_iota(jnp.int32, (2 * heads * rows, heads * QB), 0)
        col = lax.broadcasted_iota(jnp.int32, (2 * heads * rows, heads * QB), 1)
        wanted = (row % rows) == query_tokens[:, b * heads * QB : (b + 1) * heads * QB] - me * rows
        same = ((row // rows) % heads) == col // QB
        spread.append(jnp.transpose((wanted & same).astype(F32)).astype(BF16))

    lax.fori_loop(1, count, wait1, 0)
    step = max(1, 16 // rows)
    for p in range(part // 16):
        at_l = recv1[:, p * 16 : p * 16 + 16, :].astype(F32)
        at_r = recv1[:, part + p * 16 : part + p * 16 + 16, :].astype(F32)
        pieces = []
        for s in range(step):
            cut = slice(s * rows, (s + 1) * rows)
            l_c = at_l[:, cut].reshape(tokens, tokens)
            r_c = at_r[:, cut].reshape(tokens, tokens).astype(BF16)
            tri = dot(jnp.transpose(l_c).astype(BF16), r_c)
            pieces.append(tri.reshape(count, rows, tokens))
        send2[:, p * 16 : p * 16 + 16, :] = jnp.concatenate(pieces, axis=1).astype(BF16)
    lax.fori_loop(1, count, start2, 0)
    recv2[me] = send2[me]
    lax.fori_loop(1, count, wait2, 0)

    for q in range(chunks):
        cut = slice(q * LANES, (q + 1) * LANES)
        triangle = recv2[:, :, cut].astype(F32).reshape(width, rows, LANES)
        flat_l[q] = layer_norm(triangle, 0).reshape(width * rows, LANES)
    turned_bias = turned(bias_ref[...])
    bias_rows = []
    for k in range(rows):
        for q in range(chunks):
            cut = slice(q * LANES, (q + 1) * LANES)
            tri_normed = flat_l[q, pl.ds(k, width, stride=rows), :]
            update = dot(jnp.transpose(tri_normed).astype(BF16), out_ref[...])
            result = (pair_ref[k, cut].astype(F32) + gates[k, cut] * update).astype(BF16)
            pair_out[k, cut] = result
            pair_normed = layer_norm(result.astype(F32), -1).astype(BF16)
            bias_rows.append(dot(turned_bias, pair_normed, NT))
    table = jnp.stack(
        [
            jnp.concatenate(bias_rows[k * chunks : (k + 1) * chunks], axis=1)
            for k in range(rows)
        ],
        axis=1,
    ).reshape(heads * rows, tokens)
    high = table.astype(BF16)
    low = (table - high.astype(F32)).astype(BF16)
    both = dot(jnp.concatenate([high, low], axis=0), key_hot).astype(BF16)
    parts = []
    for b in range(blocks):
        scores = base[b] + dot(spread[b], both[:, b * QB : b * QB + KB])
        powers = jnp.exp(scores - jnp.max(scores, axis=-1, keepdims=True))
        weights = (powers / jnp.sum(powers, axis=-1, keepdims=True)).astype(BF16)
        every = dot(weights, vals[b * QB : b * QB + KB])
        attended = jnp.zeros((QB, width), F32)
        for h in range(heads):
            attended = jnp.where(channel == h, every[h * QB : (h + 1) * QB], attended)
        parts.append(attended)
    gated = (gating * jnp.concatenate(parts, axis=0)).astype(BF16)
    atom_out[...] = (dot(gated, aout_ref[...]) + atom_ref[...].astype(F32)).astype(BF16)
    lax.fori_loop(1, count, drain, 0)


def per_device(
    count,
    pair_input,
    tri_projection,
    tri_gate_weight,
    tri_out_weight,
    pair_bias_weight,
    atom_input,
    atom_tokens,
    atom_in_weight,
    atom_out_weight,
):
    rows, tokens, width = pair_input.shape
    atoms = atom_input.shape[0]
    heads = pair_bias_weight.shape[1]
    share = width // count
    part = share * rows
    chunks = tokens // LANES
    total_atoms = atom_tokens.shape[0]
    first_atom = lax.axis_index("row") * atoms
    padded_tokens = jnp.pad(atom_tokens, RIM)
    key_tokens = lax.dynamic_slice_in_dim(padded_tokens, first_atom, atoms + 2 * RIM)[None]
    query_tokens = lax.dynamic_slice_in_dim(atom_tokens, first_atom, atoms)
    query_tokens = jnp.tile(query_tokens.reshape(-1, 1, QB), (1, heads, 1)).reshape(1, -1)
    vmem = pl.BlockSpec(memory_space=pltpu.VMEM)
    return pl.pallas_call(
        functools.partial(kernel, count, total_atoms),
        out_shape=(
            jax.ShapeDtypeStruct(pair_input.shape, BF16),
            jax.ShapeDtypeStruct(atom_input.shape, BF16),
        ),
        in_specs=[vmem] * 10,
        out_specs=(vmem, vmem),
        scratch_shapes=[
            pltpu.VMEM((chunks, width * rows, LANES), F32),
            pltpu.VMEM((chunks, width * rows, LANES), F32),
            pltpu.VMEM((count, 2 * part, tokens), BF16),
            pltpu.VMEM((count, 2 * part, tokens), BF16),
            pltpu.VMEM((count, part, tokens), BF16),
            pltpu.VMEM((count, part, tokens), BF16),
            pltpu.VMEM((rows, tokens, width), F32),
            pltpu.VMEM((atoms + 2 * RIM, width), BF16),
            pltpu.SemaphoreType.DMA((count,)),
            pltpu.SemaphoreType.DMA((count,)),
            pltpu.SemaphoreType.DMA((count,)),
            pltpu.SemaphoreType.DMA((count,)),
            pltpu.SemaphoreType.DMA((2,)),
            pltpu.SemaphoreType.DMA((2,)),
        ],
        compiler_params=pltpu.CompilerParams(
            collective_id=0, has_side_effects=True, vmem_limit_bytes=40 * 1024 * 1024
        ),
    )(
        pair_input,
        tri_projection,
        tri_gate_weight,
        tri_out_weight,
        pair_bias_weight,
        atom_input,
        query_tokens,
        key_tokens,
        atom_in_weight,
        atom_out_weight,
    )


def solution(mesh):
    placed = (
        P(("group", "row"), None, None),
        P(),
        P(),
        P(),
        P(),
        P(("group", "row"), None),
        P("group"),
        P(),
        P(),
    )
    return jax.shard_map(
        functools.partial(per_device, mesh.shape["row"]),
        mesh=mesh,
        in_specs=placed,
        out_specs=(P(("group", "row"), None, None), P(("group", "row"), None)),
        check_vma=False,
    )
```

time: 83.8 us -> 35.3 us (0.42)
  waiting for transfers between devices: 42.6 us -> 0 us
  Pallas kernels: 0 us -> 27.6 us
  between operations: 14.4 us -> 0.7 us
  starting transfers between devices: 11 us -> 0 us
  matrix products: 9.17 us -> 0 us
  local copies, waits for them, and re-layouts: 4.78 us -> 6.65 us
  other arithmetic: 1.49 us -> 0 us
    all_gather x1 -> x0, waiting for transfers between devices: 35.7 us -> none  [per_device(): lax.all_gather(right_side, 'row', axis=1, tiled=True)]
    pallas_call x0 -> x1, Pallas kernels: none -> 27.6 us  [per_device(): pl.pallas_call(functools.partial(kernel, count, total_atoms), out_shape=(...]
    dot_general x11 -> x0, matrix products: 9.17 us -> none  [the longest x1 5.63 us: per_device(): jnp.einsum('cki,ckj->cij', turned, lax.all_gather(right_side, 'row', axis...]
    all_to_all x1 -> x0, starting transfers between devices: 7.38 us -> none  [per_device(): lax.all_to_all(left_side, 'row', split_axis=2, concat_axis=1, tiled=True)]
    all_to_all x1 -> x0, waiting for transfers between devices: 4.86 us -> none  [per_device(): lax.all_to_all(left_side, 'row', split_axis=2, concat_axis=1, tiled=True)]
    unnamed x18 -> x21, local copies, waits for them, and re-layouts: 2.09 us -> 6.33 us
    ppermute x2 -> x0, starting transfers between devices: 3.6 us -> none  [the longest x1 2.31 us: padded(): lax.ppermute(lax.slice_in_dim(block, block.shape[dim] - width, None, axis...]
    ppermute x2 -> x0, waiting for transfers between devices: 2.05 us -> none  [the longest x1 2.05 us: padded(): lax.ppermute(lax.slice_in_dim(block, 0, width, axis=dim), axis, backward)]
  transfers between devices with their start and end apart: 4 -> 0, of which waited for: 3 -> 0; matrix products, arithmetic and copies ran while one was open for 3% -> 0% of each run, Pallas kernels for 0% -> 0%
where the time goes in v1:
time: 35.3 us; the launch traced here: 34.9 us
  Pallas kernels  27.6 us (78%)
  local copies, waits for them, and re-layouts  6.65 us (19%)
  between operations  0.7 us (2%)
    pallas_call x1, Pallas kernels, per_device(): pl.pallas_call(functools.partial(kernel, count, total_atoms), out_shape=(...  27.6 us
    unnamed x21, local copies, waits for them, and re-layouts  6.33 us

profile of v1, /device:TPU:0, one launch (start us, length us, event | category | flops | bytes accessed | tf_op | source)
XLA Modules:
  0.0 34.9 jit_solution(866242026842274954)
XLA Ops:
  0.6 0.0 copy-start.7
  0.6 0.0 copy-start.8
  0.7 0.0 copy-start.4
  0.7 0.0 copy-start.3
  0.7 0.6 %copy-done.7 = s32[1024]{0:T(1024)S(1)} copy-done((s32[1024]{0:T(1024)S(1)}, s32[1024]{0:T(1024)}, u32[]{:S(2)}) %copy-start.7) | copy-done | bytes 4120
  1.3 0.1 dynamic_slice.6
  1.4 0.1 tile.9
  1.5 0.1 pad_dynamic-slice_fusion
  1.6 0.1 tile.11.qtok_ref
  1.6 0.0 copy-done.8
  1.6 0.1 copy.11.bias_ref
  1.8 0.0 copy-done.4
  1.8 0.0 copy-done.3
  1.8 0.0 copy-start
  1.8 0.9 %copy-done = bf16[8,128,128]{2,1,0:T(8,128)(2,1)S(1)} copy-done((bf16[8,128,128]{2,1,0:T(8,128)(2,1)S(1)}, bf16[8,128,128]{2,1,0:T(8,128)(2,1)}, u32[]{:S(2)}) %copy-start) | copy-done | bytes 262168
  2.7 0.9 %copy-done.1 = bf16[128,512]{1,0:T(8,128)(2,1)S(1)} copy-done((bf16[128,512]{1,0:T(8,128)(2,1)S(1)}, bf16[128,512]{1,0:T(8,128)(2,1)}, u32[]{:S(2)}) %copy-start.1) | copy-done | bytes 131096
  3.7 0.0 copy-start.2
  3.7 0.9 %copy-done.2 = bf16[128,512]{1,0:T(8,128)(2,1)S(1)} copy-done((bf16[128,512]{1,0:T(8,128)(2,1)S(1)}, bf16[128,512]{1,0:T(8,128)(2,1)}, u32[]{:S(2)}) %copy-start.2) | copy-done | bytes 131096
  4.6 0.0 copy-start.5
  4.6 0.8 %copy-done.5 = bf16[128,128]{1,0:T(8,128)(2,1)S(1)} copy-done((bf16[128,128]{1,0:T(8,128)(2,1)S(1)}, bf16[128,128]{1,0:T(8,128)(2,1)}, u32[]{:S(2)}) %copy-start.5) | copy-done | bytes 32792
  5.3 0.7 %copy-done.6 = bf16[64,128]{1,0:T(8,128)(2,1)S(1)} copy-done((bf16[64,128]{1,0:T(8,128)(2,1)S(1)}, bf16[64,128]{1,0:T(8,128)(2,1)}, u32[]{:S(2)}) %copy-start.6) | copy-done | bytes 16408
  6.0 27.6 %shard_map.104 = (bf16[8,128,128]{2,1,0:T(8,128)(2,1)S(1)}, bf16[64,128]{1,0:T(8,128)(2,1)S(1)}) custom-call(bf16[8,128,128]{2,1,0:T(8,128)(2,1)S(1)} %copy-done, bf16[128,512]{1,0:T(8,128)(2,1)S(1)} %copy-done.1, bf16[128,128]{1,0:T(8,128)(2,1)S(1)} %copy-done.3, bf16[128,128]{1,0:T(8,128)(2,1)S(1)} %copy-done.4, bf16[128,4]{1,0:T(8,128)(2,1)S(1)} %copy.11.bias_ref, ...), custom_call_target="tpu_custom_call" | custom-call | tf_op jit(solution)/shard_map/pallas_call | solution.py:284
  33.6 0.7 %copy.14 = bf16[8,128,128]{2,1,0:T(8,128)(2,1)} copy(bf16[8,128,128]{2,1,0:T(8,128)(2,1)S(1)} %get-tuple-element.4) | data formatting | bytes 524288
  34.3 0.6 %copy.15 = bf16[64,128]{1,0:T(8,128)(2,1)} copy(bf16[64,128]{1,0:T(8,128)(2,1)S(1)} %get-tuple-element.5) | data formatting | bytes 32768
  (3 shorter events, 0.0 us)
Async XLA Ops:
  0.6 0.7 %copy-start.7 = (s32[1024]{0:T(1024)S(1)}, s32[1024]{0:T(1024)}, u32[]{:S(2)}) copy-start(s32[1024]{0:T(1024)} %param.15) | copy-start | bytes 12292
  0.6 1.0 %copy-start.8 = (bf16[128,4]{0,1:T(4,128)(2,1)S(1)}, bf16[128,4]{0,1:T(4,128)(2,1)}, u32[]{:S(2)}) copy-start(bf16[128,4]{0,1:T(4,128)(2,1)} %param.13) | copy-start | bytes 3076
  0.7 1.1 %copy-start.4 = (bf16[128,128]{1,0:T(8,128)(2,1)S(1)}, bf16[128,128]{1,0:T(8,128)(2,1)}, u32[]{:S(2)}) copy-start(bf16[128,128]{1,0:T(8,128)(2,1)} %out_ref.1) | copy-start | bytes 98308
  0.7 1.1 %copy-start.3 = (bf16[128,128]{1,0:T(8,128)(2,1)S(1)}, bf16[128,128]{1,0:T(8,128)(2,1)}, u32[]{:S(2)}) copy-start(bf16[128,128]{1,0:T(8,128)(2,1)} %gate_ref.1) | copy-start | bytes 98308
  1.8 1.0 %copy-start = (bf16[8,128,128]{2,1,0:T(8,128)(2,1)S(1)}, bf16[8,128,128]{2,1,0:T(8,128)(2,1)}, u32[]{:S(2)}) copy-start(bf16[8,128,128]{2,1,0:T(8,128)(2,1)} %pair_ref.1) | copy-start | bytes 786436
  2.7 0.9 %copy-start.1 = (bf16[128,512]{1,0:T(8,128)(2,1)S(1)}, bf16[128,512]{1,0:T(8,128)(2,1)}, u32[]{:S(2)}) copy-start(bf16[128,512]{1,0:T(8,128)(2,1)} %proj_ref.1) | copy-start | bytes 393220
  3.7 0.9 %copy-start.2 = (bf16[128,512]{1,0:T(8,128)(2,1)S(1)}, bf16[128,512]{1,0:T(8,128)(2,1)}, u32[]{:S(2)}) copy-start(bf16[128,512]{1,0:T(8,128)(2,1)} %ain_ref.1) | copy-start | bytes 393220
  4.6 0.8 %copy-start.5 = (bf16[128,128]{1,0:T(8,128)(2,1)S(1)}, bf16[128,128]{1,0:T(8,128)(2,1)}, u32[]{:S(2)}) copy-start(bf16[128,128]{1,0:T(8,128)(2,1)} %aout_ref.1) | copy-start | bytes 98308
  5.3 0.7 %copy-start.6 = (bf16[64,128]{1,0:T(8,128)(2,1)S(1)}, bf16[64,128]{1,0:T(8,128)(2,1)}, u32[]{:S(2)}) copy-start(bf16[64,128]{1,0:T(8,128)(2,1)} %atom_ref.1) | copy-start | bytes 49156

commit v2 on v1

v2 whole, which is shorter than its diff:
```python
import functools

import jax
import jax.numpy as jnp
from jax import lax
from jax.experimental import pallas as pl
from jax.experimental.pallas import tpu as pltpu
from jax.sharding import PartitionSpec as P

QB = 32
KB = 128
RIM = 48
LANES = 128
NORM_EPSILON = 1e-05
F32 = jnp.float32
BF16 = jnp.bfloat16
NN = (((1,), (0,)), ((), ()))
NT = (((1,), (1,)), ((), ()))


def dot(a, b, dims=NN):
    return lax.dot_general(a, b, dims, preferred_element_type=F32)


def turned(x):
    return jnp.transpose(x.astype(F32)).astype(BF16)


def layer_norm(values, axis):
    average = jnp.mean(values, axis=axis, keepdims=True)
    centred = values - average
    variance = jnp.mean(centred * centred, axis=axis, keepdims=True)
    return centred * lax.rsqrt(variance + NORM_EPSILON)


def kernel(
    count,
    groups,
    total_atoms,
    pair_hbm,
    proj_hbm,
    gate_hbm,
    out_hbm,
    bias_ref,
    atom_hbm,
    tok_hbm,
    ain_hbm,
    aout_hbm,
    pair_out,
    atom_out,
    pair_ref,
    proj_ref,
    gate_ref,
    out_ref,
    tok_ref,
    ain_ref,
    aout_ref,
    normed_ref,
    flat_l,
    flat_r,
    send1,
    recv1,
    send2,
    recv2,
    gates,
    ext,
    ssem1,
    rsem1,
    ssem2,
    rsem2,
    hsem_s,
    hsem_r,
    isem,
):
    rows, tokens, width = pair_ref.shape
    share = width // count
    part = share * rows // groups
    held = width // groups
    chunks = tokens // LANES
    atoms = ext.shape[0] - 2 * RIM
    reach = atoms + 2 * RIM
    heads = bias_ref.shape[0]
    head_size = width // heads
    blocks = atoms // QB
    token_rows = total_atoms // LANES
    me = lax.axis_index("row")
    right = lax.rem(me + 1, count)
    left = lax.rem(me + count - 1, count)
    cuts = [slice(q * LANES, (q + 1) * LANES) for q in range(chunks)]

    barrier = pltpu.get_barrier_semaphore()

    def greet(step, carry):
        pl.semaphore_signal(barrier, inc=1, device_id={"row": lax.rem(me + step, count)})
        return carry

    lax.fori_loop(1, count, greet, 0)

    fetches = [
        pltpu.make_async_copy(source, target, isem.at[i])
        for i, (source, target) in enumerate(
            [
                (pair_hbm, pair_ref),
                (proj_hbm, proj_ref),
                (gate_hbm, gate_ref),
                (out_hbm, out_ref),
                (atom_hbm, ext.at[pl.ds(RIM, atoms)]),
                (tok_hbm, tok_ref.at[pl.ds(8, token_rows)]),
                (ain_hbm, ain_ref),
                (aout_hbm, aout_ref),
            ]
        )
    ]
    for fetch in fetches:
        fetch.start()
    tok_ref[pl.ds(0, 8), :] = jnp.zeros((8, LANES), jnp.int32)
    tok_ref[pl.ds(8 + token_rows, 8), :] = jnp.zeros((8, LANES), jnp.int32)

    def peer_of(step):
        return lax.rem(me + lax.rem(step + count // 2 - 2, count - 1) + 1, count)

    def halo(side):
        source = atom_hbm.at[pl.ds(atoms - RIM, RIM)] if side == 0 else atom_hbm.at[pl.ds(0, RIM)]
        target = ext.at[pl.ds(0, RIM)] if side == 0 else ext.at[pl.ds(RIM + atoms, RIM)]
        return pltpu.make_async_remote_copy(
            src_ref=source,
            dst_ref=target,
            send_sem=hsem_s.at[side],
            recv_sem=hsem_r.at[side],
            device_id={"row": right if side == 0 else left},
        )

    def copy1(g, peer, slot):
        return pltpu.make_async_remote_copy(
            src_ref=send1.at[g, peer],
            dst_ref=recv1.at[g, slot],
            send_sem=ssem1.at[g, peer],
            recv_sem=rsem1.at[g, slot],
            device_id={"row": peer},
        )

    def copy2(g, peer, slot):
        return pltpu.make_async_remote_copy(
            src_ref=send2.at[g, peer],
            dst_ref=recv2.at[g, slot],
            send_sem=ssem2.at[g, peer],
            recv_sem=rsem2.at[g, slot],
            device_id={"row": peer},
        )

    def start(copy, g):
        def body(step, carry):
            copy(g, peer_of(step), me).start()
            return carry

        lax.fori_loop(1, count, body, 0)

    def arrive(copy, g):
        def body(step, carry):
            peer = peer_of(step)
            copy(g, peer, peer).wait_recv()
            return carry

        lax.fori_loop(1, count, body, 0)

    def leave(copy, g):
        def body(step, carry):
            peer = peer_of(step)
            copy(g, peer, peer).wait_send()
            return carry

        lax.fori_loop(1, count, body, 0)

    fetches[1].wait()
    turned_proj = turned(proj_ref[...])
    fetches[0].wait()
    for g in range(groups):
        sides = [
            turned_proj[t * width + g * held : t * width + (g + 1) * held] for t in range(4)
        ]
        sides = jnp.concatenate(sides, axis=0)
        for k in range(rows):
            if g == 0:
                normed = layer_norm(pair_ref[k].astype(F32), -1).astype(BF16)
                normed_ref[k] = normed
            else:
                normed = normed_ref[k]
            projected = dot(sides, normed, NT)
            left_side = jax.nn.sigmoid(projected[held : 2 * held]) * projected[:held]
            right_side = jax.nn.sigmoid(projected[3 * held :]) * projected[2 * held : 3 * held]
            for q in range(chunks):
                flat_l[q, pl.ds(g * held * rows + k, held, stride=rows), :] = left_side[:, cuts[q]]
                flat_r[q, pl.ds(g * held * rows + k, held, stride=rows), :] = right_side[:, cuts[q]]
        span = pl.ds(g * held * rows, held * rows)
        for q in range(chunks):
            send1[g, :, :part, cuts[q]] = (
                flat_l[q, span, :].reshape(count, part, LANES).astype(BF16)
            )
            send1[g, :, part:, cuts[q]] = (
                flat_r[q, span, :].reshape(count, part, LANES).astype(BF16)
            )
        if g == 0:
            pl.semaphore_wait(barrier, count - 1)
            halo(0).start()
            halo(1).start()
        start(copy1, g)
        recv1[g, me] = send1[g, me]

    fetches[2].wait()
    for k in range(rows):
        gates[k] = jax.nn.sigmoid(dot(normed_ref[k], gate_ref[...]))

    for i in (3, 4, 5, 6, 7):
        fetches[i].wait()
    halo(0).wait()
    halo(1).wait()
    atom_normed = layer_norm(ext[...].astype(F32), -1).astype(BF16)
    atom_proj = dot(atom_normed, ain_ref[...])
    own = atom_proj[RIM : RIM + atoms]
    queries = (own[:, :width] * head_size ** (-0.5)).astype(BF16)
    gating = jax.nn.sigmoid(own[:, 3 * width :])
    keys = atom_proj[:, width : 2 * width].astype(BF16)
    vals = atom_proj[:, 2 * width : 3 * width].astype(BF16)
    channel = lax.broadcasted_iota(jnp.int32, (QB, width), 1) // head_size
    first_atom = me * atoms
    token_row = first_atom // LANES
    around = jnp.concatenate(
        [tok_ref[pl.ds(7 + token_row + t, 1), :] for t in range(3)], axis=1
    )
    key_tokens = around[:, LANES - RIM : LANES - RIM + reach]
    for t in range(1, LANES // atoms):
        begin = LANES - RIM + t * atoms
        key_tokens = jnp.where(
            first_atom % LANES == t * atoms, around[:, begin : begin + reach], key_tokens
        )
    key_hot = (lax.broadcasted_iota(jnp.int32, (tokens, reach), 0) == key_tokens).astype(BF16)
    base = []
    spread = []
    for b in range(blocks):
        q_b = queries[b * QB : (b + 1) * QB]
        q_all = jnp.concatenate(
            [jnp.where(channel == h, q_b, jnp.zeros_like(q_b)) for h in range(heads)], axis=0
        )
        scores = dot(q_all, keys[b * QB : b * QB + KB], NT)
        position = (
            first_atom
            + (b * QB - RIM)
            + lax.broadcasted_iota(jnp.int32, (heads * QB, KB), 1)
        )
        inside = (position >= 0) & (position < total_atoms)
        base.append(jnp.where(inside, scores, -jnp.inf))
        row = lax.broadcasted_iota(jnp.int32, (2 * heads * rows, heads * QB), 0)
        col = lax.broadcasted_iota(jnp.int32, (2 * heads * rows, heads * QB), 1)
        begin = RIM + b * QB
        own_tokens = jnp.concatenate([key_tokens[:, begin : begin + QB]] * heads, axis=1)
        wanted = (row % rows) == own_tokens - me * rows
        same = ((row // rows) % heads) == col // QB
        spread.append(jnp.transpose((wanted & same).astype(F32)).astype(BF16))

    step = 16 // rows
    for g in range(groups):
        arrive(copy1, g)
        for p in range(part // 16):
            at_l = recv1[g, :, p * 16 : p * 16 + 16, :].astype(F32)
            at_r = recv1[g, :, part + p * 16 : part + p * 16 + 16, :].astype(F32)
            pieces = []
            for s in range(step):
                cut = slice(s * rows, (s + 1) * rows)
                l_c = at_l[:, cut].reshape(tokens, tokens)
                r_c = at_r[:, cut].reshape(tokens, tokens).astype(BF16)
                tri = dot(jnp.transpose(l_c).astype(BF16), r_c)
                pieces.append(tri.reshape(count, rows, tokens))
            send2[g, :, p * 16 : p * 16 + 16, :] = jnp.concatenate(pieces, axis=1).astype(BF16)
        start(copy2, g)
        recv2[g, me] = send2[g, me]
    for g in range(groups):
        arrive(copy2, g)

    for q in range(chunks):
        triangle = recv2[:, :, :, cuts[q]].astype(F32).reshape(width, rows, LANES)
        flat_l[q] = layer_norm(triangle, 0).reshape(width * rows, LANES)
    turned_bias = bias_ref[...].astype(BF16)
    bias_rows = []
    for k in range(rows):
        for cut_q in range(chunks):
            cut = cuts[cut_q]
            tri_normed = flat_l[cut_q, pl.ds(k, width, stride=rows), :]
            update = dot(jnp.transpose(tri_normed).astype(BF16), out_ref[...])
            result = (pair_ref[k, cut].astype(F32) + gates[k, cut] * update).astype(BF16)
            pair_out[k, cut] = result
            pair_normed = layer_norm(result.astype(F32), -1).astype(BF16)
            bias_rows.append(dot(turned_bias, pair_normed, NT))
    table = jnp.stack(
        [
            jnp.concatenate(bias_rows[k * chunks : (k + 1) * chunks], axis=1)
            for k in range(rows)
        ],
        axis=1,
    ).reshape(heads * rows, tokens)
    high = table.astype(BF16)
    low = (table - high.astype(F32)).astype(BF16)
    both = dot(jnp.concatenate([high, low], axis=0), key_hot).astype(BF16)
    parts = []
    for b in range(blocks):
        scores = base[b] + dot(spread[b], both[:, b * QB : b * QB + KB])
        powers = jnp.exp(scores - jnp.max(scores, axis=-1, keepdims=True))
        weights = (powers / jnp.sum(powers, axis=-1, keepdims=True)).astype(BF16)
        every = dot(weights, vals[b * QB : b * QB + KB])
        attended = jnp.zeros((QB, width), F32)
        for h in range(heads):
            attended = jnp.where(channel == h, every[h * QB : (h + 1) * QB], attended)
        parts.append(attended)
    gated = (gating * jnp.concatenate(parts, axis=0)).astype(BF16)
    atom_out[...] = (
        dot(gated, aout_ref[...]) + ext[pl.ds(RIM, atoms), :].astype(F32)
    ).astype(BF16)
    for g in range(groups):
        leave(copy1, g)
        leave(copy2, g)


def per_device(
    count,
    pair_input,
    tri_projection,
    tri_gate_weight,
    tri_out_weight,
    pair_bias_weight,
    atom_input,
    atom_tokens,
    atom_in_weight,
    atom_out_weight,
):
    rows, tokens, width = pair_input.shape
    atoms = atom_input.shape[0]
    groups = max(1, width // count * rows // 32)
    part = width // count * rows // groups
    chunks = tokens // LANES
    total_atoms = atom_tokens.shape[0]
    vmem = pl.BlockSpec(memory_space=pltpu.VMEM)
    anywhere = pl.BlockSpec(memory_space=pl.ANY)
    return pl.pallas_call(
        functools.partial(kernel, count, groups, total_atoms),
        out_shape=(
            jax.ShapeDtypeStruct(pair_input.shape, BF16),
            jax.ShapeDtypeStruct(atom_input.shape, BF16),
        ),
        in_specs=[anywhere] * 4 + [vmem] + [anywhere] * 4,
        out_specs=(vmem, vmem),
        scratch_shapes=[
            pltpu.VMEM(pair_input.shape, BF16),
            pltpu.VMEM(tri_projection.shape, BF16),
            pltpu.VMEM(tri_gate_weight.shape, BF16),
            pltpu.VMEM(tri_out_weight.shape, BF16),
            pltpu.VMEM((total_atoms // LANES + 16, LANES), jnp.int32),
            pltpu.VMEM(atom_in_weight.shape, BF16),
            pltpu.VMEM(atom_out_weight.shape, BF16),
            pltpu.VMEM(pair_input.shape, BF16),
            pltpu.VMEM((chunks, width * rows, LANES), F32),
            pltpu.VMEM((chunks, width * rows, LANES), F32),
            pltpu.VMEM((groups, count, 2 * part, tokens), BF16),
            pltpu.VMEM((groups, count, 2 * part, tokens), BF16),
            pltpu.VMEM((groups, count, part, tokens), BF16),
            pltpu.VMEM((groups, count, part, tokens), BF16),
            pltpu.VMEM((rows, tokens, width), F32),
            pltpu.VMEM((atoms + 2 * RIM, width), BF16),
            pltpu.SemaphoreType.DMA((groups, count)),
            pltpu.SemaphoreType.DMA((groups, count)),
            pltpu.SemaphoreType.DMA((groups, count)),
            pltpu.SemaphoreType.DMA((groups, count)),
            pltpu.SemaphoreType.DMA((2,)),
            pltpu.SemaphoreType.DMA((2,)),
            pltpu.SemaphoreType.DMA((8,)),
        ],
        compiler_params=pltpu.CompilerParams(
            collective_id=0, has_side_effects=True, vmem_limit_bytes=60 * 1024 * 1024
        ),
    )(
        pair_input,
        tri_projection,
        tri_gate_weight,
        tri_out_weight,
        pair_bias_weight.T.astype(F32),
        atom_input,
        atom_tokens.reshape(-1, LANES),
        atom_in_weight,
        atom_out_weight,
    )


def solution(mesh):
    placed = (
        P(("group", "row"), None, None),
        P(),
        P(),
        P(),
        P(),
        P(("group", "row"), None),
        P("group"),
        P(),
        P(),
    )
    return jax.shard_map(
        functools.partial(per_device, mesh.shape["row"]),
        mesh=mesh,
        in_specs=placed,
        out_specs=(P(("group", "row"), None, None), P(("group", "row"), None)),
        check_vma=False,
    )
```

time: 35.3 us -> 37.4 us (1.059)
  Pallas kernels: 27.6 us -> 33 us
  local copies, waits for them, and re-layouts: 6.65 us -> 2.96 us
  other arithmetic: 0 us -> 0.58 us
    pallas_call x1, Pallas kernels: 27.6 us -> 33 us  [per_device(): pl.pallas_call(functools.partial(kernel, count, groups, total_atoms), out...]
    unnamed x21 -> x6, local copies, waits for them, and re-layouts: 6.33 us -> 2.96 us
    convert_element_type x0 -> x1, other arithmetic: none -> 0.58 us  [per_device(): pair_bias_weight.T.astype(F32)]
where the time goes in v2:
time: 37.4 us; the launch traced here: 37.2 us
  Pallas kernels  33 us (88%)
  local copies, waits for them, and re-layouts  2.96 us (8%)
  between operations  0.66 us (2%)
  other arithmetic  0.58 us (2%)
    pallas_call x1, Pallas kernels, per_device(): pl.pallas_call(functools.partial(kernel, count, groups, total_atoms), out...  33 us
    unnamed x6, local copies, waits for them, and re-layouts  2.96 us

profile of v2, /device:TPU:0, one launch (start us, length us, event | category | flops | bytes accessed | tf_op | source)
XLA Modules:
  0.0 37.2 jit_solution(441067692575077503)
XLA Ops:
  0.6 0.0 copy-start.1
  0.6 0.7 %copy-done.1 = bf16[128,4]{0,1:T(4,128)(2,1)S(1)} copy-done((bf16[128,4]{0,1:T(4,128)(2,1)S(1)}, bf16[128,4]{0,1:T(4,128)(2,1)}, u32[]{:S(2)}) %copy-start.1) | copy-done | bytes 1048
  1.3 0.6 %convert_bitcast_fusion.bias_ref = f32[4,128]{1,0:T(4,128)} fusion(bf16[128,4]{0,1:T(4,128)(2,1)S(1)} %copy-done.1), kind=kLoop, calls=%fused_computation | loop fusion | flops 512 | bytes 3072 | tf_op jit(solution)/shard_map/convert_element_type | solution.py:383
  1.9 33.0 %shard_map.104 = (bf16[8,128,128]{2,1,0:T(8,128)(2,1)}, bf16[64,128]{1,0:T(8,128)(2,1)}) custom-call(bf16[8,128,128]{2,1,0:T(8,128)(2,1)} %pair_hbm.1, bf16[128,512]{1,0:T(8,128)(2,1)} %proj_hbm.1, bf16[128,128]{1,0:T(8,128)(2,1)} %gate_hbm.1, bf16[128,128]{1,0:T(8,128)(2,1)} %out_hbm.1, f32[4,128]{1,0:T(4,128)} %convert_bitcast_fusion.bias_ref, ...), custom_call_target="tpu_custom_call" | custom-call | tf_op jit(solution)/shard_map/pallas_call | solution.py:342
  34.9 0.0 copy-start
  34.9 1.7 %copy.13 = bf16[8,128,128]{2,1,0:T(8,128)(2,1)} copy(bf16[8,128,128]{2,1,0:T(8,128)(2,1)} %get-tuple-element.4) | data formatting | bytes 524288
  36.6 0.0 copy-done
  36.6 0.6 %copy.14 = bf16[64,128]{1,0:T(8,128)(2,1)} copy(bf16[64,128]{1,0:T(8,128)(2,1)S(1)} %copy-done) | data formatting | bytes 32768
Async XLA Ops:
  0.6 0.7 %copy-start.1 = (bf16[128,4]{0,1:T(4,128)(2,1)S(1)}, bf16[128,4]{0,1:T(4,128)(2,1)}, u32[]{:S(2)}) copy-start(bf16[128,4]{0,1:T(4,128)(2,1)} %param.13) | copy-start | bytes 3076
  34.9 1.7 %copy-start = (bf16[64,128]{1,0:T(8,128)(2,1)S(1)}, bf16[64,128]{1,0:T(8,128)(2,1)}, u32[]{:S(2)}) copy-start(bf16[64,128]{1,0:T(8,128)(2,1)} %get-tuple-element.5) | copy-start | bytes 49156

commit v3 on v2

--- a/solution.py
+++ b/solution.py
@@ -41,17 +41,20 @@
     proj_hbm,
     gate_hbm,
     out_hbm,
-    bias_ref,
+    bias_hbm,
     atom_hbm,
     tok_hbm,
     ain_hbm,
     aout_hbm,
+    pair_to,
+    atom_to,
     pair_out,
     atom_out,
     pair_ref,
     proj_ref,
     gate_ref,
     out_ref,
+    bias_ref,
     tok_ref,
     ain_ref,
     aout_ref,
@@ -71,6 +74,7 @@
     hsem_s,
     hsem_r,
     isem,
+    osem,
 ):
     rows, tokens, width = pair_ref.shape
     share = width // count
@@ -94,7 +98,7 @@
         pl.semaphore_signal(barrier, inc=1, device_id={"row": lax.rem(me + step, count)})
         return carry
 
-    lax.fori_loop(1, count, greet, 0)
+    lax.fori_loop(1, count, greet, 0, unroll=True)
 
     fetches = [
         pltpu.make_async_copy(source, target, isem.at[i])
@@ -108,6 +112,7 @@
                 (tok_hbm, tok_ref.at[pl.ds(8, token_rows)]),
                 (ain_hbm, ain_ref),
                 (aout_hbm, aout_ref),
+                (bias_hbm, bias_ref),
             ]
         )
     ]
@@ -117,7 +122,7 @@
     tok_ref[pl.ds(8 + token_rows, 8), :] = jnp.zeros((8, LANES), jnp.int32)
 
     def peer_of(step):
-        return lax.rem(me + lax.rem(step + count // 2 - 2, count - 1) + 1, count)
+        return lax.rem(me + step, count)
 
     def halo(side):
         source = atom_hbm.at[pl.ds(atoms - RIM, RIM)] if side == 0 else atom_hbm.at[pl.ds(0, RIM)]
@@ -134,8 +139,8 @@
         return pltpu.make_async_remote_copy(
             src_ref=send1.at[g, peer],
             dst_ref=recv1.at[g, slot],
-            send_sem=ssem1.at[g, peer],
-            recv_sem=rsem1.at[g, slot],
+            send_sem=ssem1.at[g],
+            recv_sem=rsem1.at[g],
             device_id={"row": peer},
         )
 
@@ -143,8 +148,8 @@
         return pltpu.make_async_remote_copy(
             src_ref=send2.at[g, peer],
             dst_ref=recv2.at[g, slot],
-            send_sem=ssem2.at[g, peer],
-            recv_sem=rsem2.at[g, slot],
+            send_sem=ssem2.at[g],
+            recv_sem=rsem2.at[g],
             device_id={"row": peer},
         )
 
@@ -153,23 +158,25 @@
             copy(g, peer_of(step), me).start()
             return carry
 
-        lax.fori_loop(1, count, body, 0)
-
-    def arrive(copy, g):
-        def body(step, carry):
-            peer = peer_of(step)
-            copy(g, peer, peer).wait_recv()
-            return carry
-
-        lax.fori_loop(1, count, body, 0)
-
-    def leave(copy, g):
-        def body(step, carry):
-            peer = peer_of(step)
-            copy(g, peer, peer).wait_send()
-            return carry
-
-        lax.fori_loop(1, count, body, 0)
+        lax.fori_loop(1, count, body, 0, unroll=True)
+
+    def all1(g):
+        return pltpu.make_async_remote_copy(
+            src_ref=send1.at[g, pl.ds(0, count - 1)],
+            dst_ref=recv1.at[g, pl.ds(0, count - 1)],
+            send_sem=ssem1.at[g],
+            recv_sem=rsem1.at[g],
+            device_id={"row": right},
+        )
+
+    def all2(g):
+        return pltpu.make_async_remote_copy(
+            src_ref=send2.at[g, pl.ds(0, count - 1)],
+            dst_ref=recv2.at[g, pl.ds(0, count - 1)],
+            send_sem=ssem2.at[g],
+            recv_sem=rsem2.at[g],
+            device_id={"row": right},
+        )
 
     fetches[1].wait()
     turned_proj = turned(proj_ref[...])
@@ -210,7 +217,7 @@
     for k in range(rows):
         gates[k] = jax.nn.sigmoid(dot(normed_ref[k], gate_ref[...]))
 
-    for i in (3, 4, 5, 6, 7):
+    for i in (3, 4, 5, 6, 7, 8):
         fetches[i].wait()
     halo(0).wait()
     halo(1).wait()
@@ -259,7 +266,7 @@
 
     step = 16 // rows
     for g in range(groups):
-        arrive(copy1, g)
+        all1(g).wait_recv()
         for p in range(part // 16):
             at_l = recv1[g, :, p * 16 : p * 16 + 16, :].astype(F32)
             at_r = recv1[g, :, part + p * 16 : part + p * 16 + 16, :].astype(F32)
@@ -274,13 +281,14 @@
         start(copy2, g)
         recv2[g, me] = send2[g, me]
     for g in range(groups):
-        arrive(copy2, g)
+        all2(g).wait_recv()
 
     for q in range(chunks):
         triangle = recv2[:, :, :, cuts[q]].astype(F32).reshape(width, rows, LANES)
         flat_l[q] = layer_norm(triangle, 0).reshape(width * rows, LANES)
-    turned_bias = bias_ref[...].astype(BF16)
+    turned_bias = bias_ref[...]
     bias_rows = []
+    stores = []
     for k in range(rows):
         for cut_q in range(chunks):
             cut = cuts[cut_q]
@@ -290,6 +298,8 @@
             pair_out[k, cut] = result
             pair_normed = layer_norm(result.astype(F32), -1).astype(BF16)
             bias_rows.append(dot(turned_bias, pair_normed, NT))
+        stores.append(pltpu.make_async_copy(pair_out.at[k], pair_to.at[k], osem.at[k]))
+        stores[-1].start()
     table = jnp.stack(
         [
             jnp.concatenate(bias_rows[k * chunks : (k + 1) * chunks], axis=1)
@@ -314,9 +324,13 @@
     atom_out[...] = (
         dot(gated, aout_ref[...]) + ext[pl.ds(RIM, atoms), :].astype(F32)
     ).astype(BF16)
+    stores.append(pltpu.make_async_copy(atom_out, atom_to, osem.at[rows]))
+    stores[-1].start()
     for g in range(groups):
-        leave(copy1, g)
-        leave(copy2, g)
+        all1(g).wait_send()
+        all2(g).wait_send()
+    for store in stores:
+        store.wait()
 
 
 def per_device(
@@ -333,11 +347,10 @@
 ):
     rows, tokens, width = pair_input.shape
     atoms = atom_input.shape[0]
-    groups = max(1, width // count * rows // 32)
+    groups = 1
     part = width // count * rows // groups
     chunks = tokens // LANES
     total_atoms = atom_tokens.shape[0]
-    vmem = pl.BlockSpec(memory_space=pltpu.VMEM)
     anywhere = pl.BlockSpec(memory_space=pl.ANY)
     return pl.pallas_call(
         functools.partial(kernel, count, groups, total_atoms),
@@ -345,13 +358,16 @@
             jax.ShapeDtypeStruct(pair_input.shape, BF16),
             jax.ShapeDtypeStruct(atom_input.shape, BF16),
         ),
-        in_specs=[anywhere] * 4 + [vmem] + [anywhere] * 4,
-        out_specs=(vmem, vmem),
+        in_specs=[anywhere] * 9,
+        out_specs=(anywhere, anywhere),
         scratch_shapes=[
+            pltpu.VMEM(pair_input.shape, BF16),
+            pltpu.VMEM(atom_input.shape, BF16),
             pltpu.VMEM(pair_input.shape, BF16),
             pltpu.VMEM(tri_projection.shape, BF16),
             pltpu.VMEM(tri_gate_weight.shape, BF16),
             pltpu.VMEM(tri_out_weight.shape, BF16),
+            pltpu.VMEM(pair_bias_weight.shape[::-1], BF16),
             pltpu.VMEM((total_atoms // LANES + 16, LANES), jnp.int32),
             pltpu.VMEM(atom_in_weight.shape, BF16),
             pltpu.VMEM(atom_out_weight.shape, BF16),
@@ -364,13 +380,14 @@
             pltpu.VMEM((groups, count, part, tokens), BF16),
             pltpu.VMEM((rows, tokens, width), F32),
             pltpu.VMEM((atoms + 2 * RIM, width), BF16),
-            pltpu.SemaphoreType.DMA((groups, count)),
-            pltpu.SemaphoreType.DMA((groups, count)),
-            pltpu.SemaphoreType.DMA((groups, count)),
-            pltpu.SemaphoreType.DMA((groups, count)),
+            pltpu.SemaphoreType.DMA((groups,)),
+            pltpu.SemaphoreType.DMA((groups,)),
+            pltpu.SemaphoreType.DMA((groups,)),
+            pltpu.SemaphoreType.DMA((groups,)),
             pltpu.SemaphoreType.DMA((2,)),
             pltpu.SemaphoreType.DMA((2,)),
-            pltpu.SemaphoreType.DMA((8,)),
+            pltpu.SemaphoreType.DMA((9,)),
+            pltpu.SemaphoreType.DMA((rows + 1,)),
         ],
         compiler_params=pltpu.CompilerParams(
             collective_id=0, has_side_effects=True, vmem_limit_bytes=60 * 1024 * 1024
@@ -380,7 +397,7 @@
         tri_projection,
         tri_gate_weight,
         tri_out_weight,
-        pair_bias_weight.T.astype(F32),
+        pair_bias_weight.T,
         atom_input,
         atom_tokens.reshape(-1, LANES),
         atom_in_weight,

time: 37.4 us -> 30.8 us (0.82)
  Pallas kernels: 33 us -> 27.8 us
  local copies, waits for them, and re-layouts: 2.96 us -> 2.29 us
  other arithmetic: 0.58 us -> 0 us
    pallas_call x1, Pallas kernels: 33 us -> 27.8 us  [per_device(): pl.pallas_call(functools.partial(kernel, count, groups, total_atoms), out...]
    unnamed x6 -> x4, local copies, waits for them, and re-layouts: 2.96 us -> 2.29 us
    convert_element_type x1 -> x0, other arithmetic: 0.58 us -> none  [per_device(): pair_bias_weight.T.astype(F32)]
where the time goes in v3:
time: 30.8 us; the launch traced here: 30.7 us
  Pallas kernels  27.8 us (90%)
  local copies, waits for them, and re-layouts  2.29 us (7%)
  between operations  0.65 us (2%)
    pallas_call x1, Pallas kernels, per_device(): pl.pallas_call(functools.partial(kernel, count, groups, total_atoms), out...  27.8 us
    unnamed x4, local copies, waits for them, and re-layouts  2.29 us

profile of v3, /device:TPU:0, one launch (start us, length us, event | category | flops | bytes accessed | tf_op | source)
XLA Modules:
  0.0 30.7 jit_solution(10569326157894438969)
XLA Ops:
  0.6 27.8 %shard_map.104 = (bf16[8,128,128]{2,1,0:T(8,128)(2,1)}, bf16[64,128]{1,0:T(8,128)(2,1)}) custom-call(bf16[8,128,128]{2,1,0:T(8,128)(2,1)} %pair_hbm.1, bf16[128,512]{1,0:T(8,128)(2,1)} %proj_hbm.1, bf16[128,128]{1,0:T(8,128)(2,1)} %gate_hbm.1, bf16[128,128]{1,0:T(8,128)(2,1)} %out_hbm.1, bf16[4,128]{1,0:T(4,128)(2,1)} %bitcast.3, bf16[64,128]{1,0:T(8,128)(2,1)} %atom_hbm.1, ...), custom_call_target="tpu_custom_call" | custom-call | tf_op jit(solution)/shard_map/pallas_call | solution.py:355
  28.4 0.0 copy-start
  28.4 1.7 %copy.13 = bf16[8,128,128]{2,1,0:T(8,128)(2,1)} copy(bf16[8,128,128]{2,1,0:T(8,128)(2,1)} %get-tuple-element.4) | data formatting | bytes 524288
  30.1 0.0 copy-done
  30.1 0.6 %copy.14 = bf16[64,128]{1,0:T(8,128)(2,1)} copy(bf16[64,128]{1,0:T(8,128)(2,1)S(1)} %copy-done) | data formatting | bytes 32768
Async XLA Ops:
  28.4 1.7 %copy-start = (bf16[64,128]{1,0:T(8,128)(2,1)S(1)}, bf16[64,128]{1,0:T(8,128)(2,1)}, u32[]{:S(2)}) copy-start(bf16[64,128]{1,0:T(8,128)(2,1)} %get-tuple-element.5) | copy-start | bytes 49156
